TPU v7x, 32 devices: a whole 2x2x4 slice. The times are simulated.
32 devices in a mesh: groups: 2 (over y), gx: 8 (over z, x), gy: 2 (over core).
Axes of the slice: x: 2, y: 2, z: 4, core: 2. Of those that a mesh axis runs over, the one named last changes fastest.
Arguments:
- activations: bfloat16 [1024, 2, 4096], P('groups', 'gy', 'gx'), parts along dimension 0, may hold values from -6 to 6
- gate_weight: bfloat16 [8192, 26624], P('gy', 'gx'), may hold values from -0.0625 to 0.0625
- up_weight: bfloat16 [8192, 26624], P('gy', 'gx'), may hold values from -0.0625 to 0.0625
Outputs:
- hidden: bfloat16 [1024, 26624], P(('groups', 'gy'), 'gx'), parts along dimension 0
There are 2 independent parts, one for each index of `groups`. A program takes and returns all parts, laid end to end along the dimension named above; an argument that names none is the same for every part. Nothing has to cross between parts.
All inputs are finite; a program needn't handle non-finite values.
Results may differ from a plain program's by a relative error of at most 0.001.
Values may be sent and summed in bfloat16 or wider, within the bound.
A program may use at most 320 MiB of HBM per device.

v0:
```python
import jax
import jax.numpy as jnp
from jax import lax
from jax.sharding import PartitionSpec as P


def gated(gate, up):
    return (jax.nn.silu(gate) * up).astype(jnp.bfloat16)


def shards(activations, gate_weight, up_weight):
    rows = activations.shape[0]
    piece = lax.all_gather(activations, "gx", axis=2, tiled=True)
    count = piece.shape[2]
    flat = piece.reshape(rows, count)
    gate_rows = gate_weight
    up_rows = up_weight
    gate = jnp.dot(flat, gate_rows, preferred_element_type=jnp.float32)
    up = jnp.dot(flat, up_rows, preferred_element_type=jnp.float32)
    gate_rows, up_rows = (
        lax.psum_scatter(gate, "gy", scatter_dimension=0, tiled=True),
        lax.psum_scatter(up, "gy", scatter_dimension=0, tiled=True),
    )
    return gated(gate_rows, up_rows)


def solution(mesh):
    placed = (P("groups", "gy", "gx"), P("gy", "gx"), P("gy", "gx"))
    return jax.shard_map(
        shards, mesh=mesh, in_specs=placed, out_specs=P(("groups", "gy"), "gx"), check_vma=False
    )
```

profile of v0, /device:TPU:1, one launch (start us, length us, event | category | flops | bytes accessed | tf_op | source)
XLA Modules:
  0.0 160.1 jit_solution(17976280346951060721)
XLA Ops:
  6.5 0.0 all-gather.2.cloned.1.call-start
  6.5 0.7 all-gather.2.cloned.1.call-update
  7.3 0.0 reduce-scatter.5.cloned.1.call-start
  7.3 78.8 %all-gather.2.cloned.1.call-done = bf16[512,1,4096]{2,0,1:T(8,128)(2,1)} async-done(((bf16[512,1,512]{2,0,1:T(8,128)(2,1)}), bf16[512,1,4096]{2,0,1:T(8,128)(2,1)}) %all-gather.2.cloned.1.call-update) | async-done | bytes 4194320 | tf_op jit(solution)/shard_map/all_gather | solution.py:13
  86.1 23.3 %fusion = f32[512,3328]{1,0:T(8,128)} fusion(bf16[4096,3328]{1,0:T(8,128)(2,1)} %param.5, bf16[512,1,4096]{2,0,1:T(8,128)(2,1)} %all-gather.2.cloned.1.call-done), kind=kOutput, calls=%fused_computation | convolution fusion | flops 13958643712 | bytes 38273024 | tf_op jit(solution)/shard_map/dot_general | solution.py:19
  109.4 0.0 reduce-scatter.5.cloned.1.call-update
  109.5 0.2 reduce-scatter.3.cloned.1.call-start
  109.7 24.5 %fusion.2 = f32[512,3328]{1,0:T(8,128)} fusion(bf16[4096,3328]{1,0:T(8,128)(2,1)} %param.4, bf16[512,1,4096]{2,0,1:T(8,128)(2,1)} %all-gather.2.cloned.1.call-done), kind=kOutput, calls=%fused_computation.2 | convolution fusion | flops 13958643712 | bytes 38273024 | tf_op jit(solution)/shard_map/dot_general | solution.py:18
  134.2 0.0 reduce-scatter.3.cloned.1.call-update
  134.2 0.0 reduce-scatter.5.cloned.1.call-done
  134.2 14.2 %reduce-scatter.3.cloned.1.call-done = f32[256,3328]{1,0:T(8,128)} async-done(((f32[512,3328]{1,0:T(8,128)}), f32[256,3328]{1,0:T(8,128)}) %reduce-scatter.3.cloned.1.call-update) | async-done | bytes 3407888 | tf_op jit(solution)/shard_map/reduce_scatter | solution.py:21
  148.4 5.2 %multiply_convert_fusion = bf16[256,3328]{1,0:T(8,128)(2,1)} fusion(f32[256,3328]{1,0:T(8,128)} %reduce-scatter.5.cloned.1.call-done, f32[256,3328]{1,0:T(8,128)} %reduce-scatter.3.cloned.1.call-done), kind=kLoop, calls=%fused_computation.4 | loop fusion | flops 5111808 | bytes 8519680 | tf_op jit(solution)/shard_map/convert_element_type | solution.py:8
Async XLA Ops:
  6.5 79.6 %all-gather.2.cloned.1.call-start = ((), (), s32[]{:S(2)}) async-start(), calls=%async_computation.2 | async-start | bytes 4718592 | tf_op jit(solution)/shard_map/all_gather | solution.py:13
  7.3 127.0 %reduce-scatter.5.cloned.1.call-start = ((), (), s32[]{:S(2)}) async-start(), calls=%async_computation.4 | async-start | bytes 10223616 | tf_op jit(solution)/shard_map/reduce_scatter | solution.py:22
  109.5 39.0 %reduce-scatter.3.cloned.1.call-start = ((), (), s32[]{:S(2)}) async-start(), calls=%async_computation.3 | async-start | bytes 10223616 | tf_op jit(solution)/shard_map/reduce_scatter | solution.py:21
Sparse Core Ops, SparseCore 0:
  9.4 76.6 all-gather.1
  109.6 14.0 reduce-scatter.4
  134.3 14.0 reduce-scatter.2
where the time goes:
time: 161 us; the launch traced here: 160 us
  waiting for transfers between devices  93.8 us (58%)
  matrix products  47.8 us (30%)
  between operations  13.1 us (8%)
  other arithmetic  5.15 us (3%)
    all_gather x1, waiting for transfers between devices, shards(): piece = lax.all_gather(activations, 'gx', axis=2, tiled=True)  78.8 us
    dot_general x1, matrix products, shards(): gate = jnp.dot(flat, gate_rows, preferred_element_type=jnp.float32)  24.5 us
    dot_general x1, matrix products, shards(): up = jnp.dot(flat, up_rows, preferred_element_type=jnp.float32)  23.3 us
    reduce_scatter x1, waiting for transfers between devices, shards(): lax.psum_scatter(gate, 'gy', scatter_dimension=0, tiled=True)  14.2 us
    convert_element_type x1, other arithmetic, gated(): return (jax.nn.silu(gate) * up).astype(jnp.bfloat16)  5.15 us
  transfers between devices with their start and end apart: 3, of which 2 were waited for; matrix products, arithmetic and copies ran while one was open for 15% of the time, Pallas kernels for 0%

commit v1 on v0

v1 whole, which is shorter than its diff:
```python
import functools

import jax
import jax.numpy as jnp
from jax import lax
from jax.experimental import pallas as pl
from jax.experimental.pallas import tpu as pltpu
from jax.sharding import PartitionSpec as P

MESH = pl.DeviceIdType.MESH
PLANES = 4
CHUNKS = 4
TILE = 256


def gated(gate, up):
    return (jax.nn.silu(gate) * up).astype(jnp.bfloat16)


def shards(activations, gate_weight, up_weight):
    rows = activations.shape[0]
    piece = lax.all_gather(activations, "gx", axis=2, tiled=True)
    count = piece.shape[2]
    flat = piece.reshape(rows, count)
    gate = jnp.dot(flat, gate_weight, preferred_element_type=jnp.float32)
    up = jnp.dot(flat, up_weight, preferred_element_type=jnp.float32)
    gate_rows, up_rows = (
        lax.psum_scatter(gate, "gy", scatter_dimension=0, tiled=True),
        lax.psum_scatter(up, "gy", scatter_dimension=0, tiled=True),
    )
    return gated(gate_rows, up_rows)


def kernel(act, wg, wu, out, x, bg, bu, acc, got, res,
           act_sem, w_sem, send_sem, recv_sem, ex_send, ex_recv, out_sem):
    rows, width = act.shape
    depth = 2 * width
    half = rows // 2
    size = rows // CHUNKS
    part = size // 2
    tiles = acc.shape[0]
    gx = lax.axis_index("gx")
    c = lax.axis_index("gy")
    z = gx // 2
    col = gx % 2
    near = (PLANES - 1 - z) // 2
    p1 = z - 1 + 2 * near
    p3 = (PLANES - 1) * near
    p2 = 6 - z - p1 - p3
    order = [z, p1, p2, p3]

    def own(r, h):
        return pltpu.make_async_copy(
            act.at[pl.ds(h * half + r * part, part), :],
            x.at[z, pl.ds(r * size + h * part, part), pl.ds(col * width, width)],
            act_sem.at[r, h],
        )

    for r in range(CHUNKS):
        for h in range(2):
            own(r, h).start()

    def weights(s):
        span = pl.ds(order[s] * depth, depth)
        return [
            pltpu.make_async_copy(wg.at[span, :], bg.at[s % 2], w_sem.at[0, s]),
            pltpu.make_async_copy(wu.at[span, :], bu.at[s % 2], w_sem.at[1, s]),
        ]

    for s in range(2):
        for copy in weights(s):
            copy.start()

    targets = [z * 2 + (1 - col), gx + 2, gx - 2]
    barrier = pltpu.get_barrier_semaphore()
    pl.semaphore_signal(barrier, inc=1, device_id={"gx": targets[0]}, device_id_type=MESH)
    pl.semaphore_signal(barrier, inc=1, device_id={"gy": 1 - c}, device_id_type=MESH)

    @pl.when(z < PLANES - 1)
    def _():
        pl.semaphore_signal(barrier, inc=1, device_id={"gx": targets[1]}, device_id_type=MESH)

    @pl.when(z > 0)
    def _():
        pl.semaphore_signal(barrier, inc=1, device_id={"gx": targets[2]}, device_id_type=MESH)

    pl.semaphore_wait(barrier, 2 + (z + 2) // 3 + (5 - z) // 3)

    def link(d, p, side, r):
        block = x.at[p, pl.ds(r * size, size), pl.ds(side * width, width)]
        b = p * 2 + side
        return pltpu.make_async_remote_copy(
            src_ref=block, dst_ref=block,
            send_sem=send_sem.at[d, b, r], recv_sem=recv_sem.at[b, r],
            device_id={"gx": targets[d]}, device_id_type=MESH,
        )

    def along(at, p, r):
        inner = ((at == 1) & (p == 0)) | ((at == 2) & (p == 3))
        outer = ((at == 0) & (p == 1)) | ((at == 3) & (p == 2))
        return inner | (outer & (r % 2 == 1))

    def routes(p, side_own, r):
        rise = (p <= z) & (z < PLANES - 1)
        fall = (p >= z) & (z > 0)
        if side_own:
            return [(1, rise), (2, fall), (0, jnp.logical_not(along(z, p, r)))]
        return [(1, rise & along(z + 1, p, r)), (2, fall & along(z - 1, p, r))]

    def forward(p, side_own, r, wait=False):
        side = col if side_own else 1 - col
        for d, cond in routes(p, side_own, r):
            @pl.when(cond)
            def _(d=d):
                if wait:
                    link(d, p, side, r).wait_send()
                else:
                    link(d, p, side, r).start()

    def arrive(p, side_own, r):
        link(0, p, col if side_own else 1 - col, r).wait_recv()

    for r in range(CHUNKS):
        for h in range(2):
            own(r, h).wait()
        forward(z, True, r)

    def product(s, first, count, j):
        lhs = x[order[s], pl.ds(first, count), :]
        cut = pl.ds(pl.multiple_of(j * TILE, TILE), TILE)
        gate = jnp.dot(lhs, bg[s % 2, :, cut], preferred_element_type=jnp.float32)
        up = jnp.dot(lhs, bu[s % 2, :, cut], preferred_element_type=jnp.float32)
        return gate, up

    def accumulate(s, first, count):
        here = pl.ds(first, count)

        def body(j, carry):
            gate, up = product(s, first, count, j)
            if s:
                acc[j, here, :TILE] += gate
                acc[j, here, TILE:] += up
            else:
                acc[j, here, :TILE] = gate
                acc[j, here, TILE:] = up
            return carry

        lax.fori_loop(0, tiles, body, 0)

    def exchange(r, j):
        return pltpu.make_async_remote_copy(
            src_ref=acc.at[j, pl.ds(r * size + (1 - c) * part, part), :],
            dst_ref=got.at[j, pl.ds(r * part, part), :],
            send_sem=ex_send.at[j, r], recv_sem=ex_recv.at[j, r],
            device_id={"gy": 1 - c}, device_id_type=MESH,
        )

    def write(r):
        span = pl.ds(r * part, part)
        return pltpu.make_async_copy(res.at[span, :], out.at[span, :], out_sem.at[r])

    def finish(r):
        def body(j, carry):
            exchange(r, j).wait_recv()
            both = acc[j, pl.ds(r * size + c * part, part), :] + got[j, pl.ds(r * part, part), :]
            cut = pl.ds(pl.multiple_of(j * TILE, TILE), TILE)
            res[pl.ds(r * part, part), cut] = gated(both[:, :TILE], both[:, TILE:])
            return carry

        lax.fori_loop(0, tiles, body, 0)
        write(r).start()

    group = 2
    for s in range(PLANES):
        for copy in weights(s):
            copy.wait()

        def chunk(r, carry, s=s):
            if s < PLANES - 1:
                arrive(order[s + 1], True, r)
                forward(order[s + 1], True, r)
            arrive(order[s], False, r)
            forward(order[s], False, r)
            return carry

        if s < PLANES - 1:
            def block(k, carry, s=s):
                for i in range(group):
                    chunk(k * group + i, 0, s)
                accumulate(s, pl.multiple_of(k * group * size, size), group * size)
                return carry

            lax.fori_loop(0, CHUNKS // group, block, 0)
            if s + 2 < PLANES:
                for copy in weights(s + 2):
                    copy.start()
        else:
            def last(r, carry, s=s):
                chunk(r, 0, s)
                accumulate(s, pl.multiple_of(r * size, size), size)

                def push(j, carry):
                    exchange(r, j).start()
                    return carry

                lax.fori_loop(0, tiles, push, 0)

                @pl.when(r > 0)
                def _():
                    finish(r - 1)
                return carry

            lax.fori_loop(0, CHUNKS, last, 0)
            finish(CHUNKS - 1)

    def drain(r, carry):
        for s in range(PLANES):
            forward(order[s], True, r, wait=True)
            forward(order[s], False, r, wait=True)

        def body(j, carry):
            exchange(r, j).wait_send()
            return carry

        lax.fori_loop(0, tiles, body, 0)
        write(r).wait()
        return carry

    lax.fori_loop(0, CHUNKS, drain, 0)


def fused(activations, gate_weight, up_weight):
    rows, _, width = activations.shape
    hidden = gate_weight.shape[1]
    tiles = hidden // TILE
    depth = 2 * width
    return pl.pallas_call(
        kernel,
        out_shape=jax.ShapeDtypeStruct((rows // 2, hidden), jnp.bfloat16),
        in_specs=[pl.BlockSpec(memory_space=pl.ANY)] * 3,
        out_specs=pl.BlockSpec(memory_space=pl.ANY),
        scratch_shapes=[
            pltpu.VMEM((PLANES, rows, depth), jnp.bfloat16),
            pltpu.VMEM((2, depth, hidden), jnp.bfloat16),
            pltpu.VMEM((2, depth, hidden), jnp.bfloat16),
            pltpu.VMEM((tiles, rows, 2 * TILE), jnp.float32),
            pltpu.VMEM((tiles, rows // 2, 2 * TILE), jnp.float32),
            pltpu.VMEM((rows // 2, hidden), jnp.bfloat16),
            pltpu.SemaphoreType.DMA((CHUNKS, 2)),
            pltpu.SemaphoreType.DMA((2, PLANES)),
            pltpu.SemaphoreType.DMA((3, 2 * PLANES, CHUNKS)),
            pltpu.SemaphoreType.DMA((2 * PLANES, CHUNKS)),
            pltpu.SemaphoreType.DMA((tiles, CHUNKS)),
            pltpu.SemaphoreType.DMA((tiles, CHUNKS)),
            pltpu.SemaphoreType.DMA((CHUNKS,)),
        ],
        compiler_params=pltpu.CompilerParams(
            collective_id=0, has_side_effects=True, vmem_limit_bytes=62 * 1024 * 1024
        ),
        cost_estimate=pl.CostEstimate(
            flops=4 * rows * PLANES * depth * hidden,
            bytes_accessed=4 * PLANES * depth * hidden,
            transcendentals=rows // 2 * hidden,
        ),
    )(activations.reshape(rows, width), gate_weight, up_weight)


def solution(mesh):
    def local(activations, gate_weight, up_weight):
        rows, _, width = activations.shape
        hidden = gate_weight.shape[1]
        fits = (
            mesh.shape["gx"] == 2 * PLANES and mesh.shape["gy"] == 2
            and width % 128 == 0 and hidden % TILE == 0 and rows % (32 * CHUNKS) == 0
        )
        return (fused if fits else shards)(activations, gate_weight, up_weight)

    placed = (P("groups", "gy", "gx"), P("gy", "gx"), P("gy", "gx"))
    return jax.shard_map(
        local, mesh=mesh, in_specs=placed, out_specs=P(("groups", "gy"), "gx"), check_vma=False
    )
```

time: 161 us -> 80.2 us (0.50)
  waiting for transfers between devices: 93.8 us -> 0 us
  Pallas kernels: 0 us -> 77.3 us
  matrix products: 47.8 us -> 0 us
  between operations: 13.1 us -> 0.01 us
  other arithmetic: 5.15 us -> 0 us
  local copies, waits for them, and re-layouts: 0 us -> 2.75 us
    all_gather x1 -> x0, waiting for transfers between devices: 78.8 us -> none  [shards(): piece = lax.all_gather(activations, 'gx', axis=2, tiled=True)]
    pallas_call x0 -> x1, Pallas kernels: none -> 77.3 us  [fused(): pl.pallas_call(kernel, out_shape=jax.ShapeDtypeStruct((rows // 2, hidden)...]
    dot_general x2 -> x0, matrix products: 47.8 us -> none  [the longest x1 24.5 us: shards(): gate = jnp.dot(flat, gate_rows, preferred_element_type=jnp.float32)]
    reduce_scatter x2 -> x0, waiting for transfers between devices: 14.2 us -> none  [the longest x1 14.2 us: shards(): lax.psum_scatter(gate, 'gy', scatter_dimension=0, tiled=True)]
    convert_element_type x1 -> x0, other arithmetic: 5.15 us -> none  [gated(): return (jax.nn.silu(gate) * up).astype(jnp.bfloat16)]
    unnamed x0 -> x1, local copies, waits for them, and re-layouts: none -> 2.75 us
  transfers between devices with their start and end apart: 3 -> 0, of which waited for: 2 -> 0; matrix products, arithmetic and copies ran while one was open for 15% -> 0% of each run, Pallas kernels for 0% -> 0%
where the time goes in v1:
time: 80.2 us; the launch traced here: 80 us
  Pallas kernels  77.3 us (96%)
  local copies, waits for them, and re-layouts  2.75 us (3%)
    pallas_call x1, Pallas kernels, fused(): pl.pallas_call(kernel, out_shape=jax.ShapeDtypeStruct((rows // 2, hidden)...  77.3 us
    unnamed x1, local copies, waits for them, and re-layouts  2.75 us

profile of v1, /device:TPU:1, one launch (start us, length us, event | category | flops | bytes accessed | tf_op | source)
XLA Modules:
  0.0 80.0 jit_solution(3067204847505882551)
XLA Ops:
  0.0 77.3 %shard_map.37 = bf16[256,3328]{1,0:T(8,128)(2,1)} custom-call(bf16[512,512]{1,0:T(8,128)(2,1)} %bitcast.1, bf16[4096,3328]{1,0:T(8,128)(2,1)} %wg.1, bf16[4096,3328]{1,0:T(8,128)(2,1)} %wu.1), custom_call_target="tpu_custom_call" | custom-call | flops 27917287424 | bytes 54525952 | tf_op jit(solution)/shard_map/pallas_call | solution.py:237
  77.3 2.7 %copy.5 = bf16[256,3328]{1,0:T(8,128)(2,1)} copy(bf16[256,3328]{1,0:T(8,128)(2,1)} %shard_map.37) | data formatting | bytes 3407872

commit v2 on v1

--- a/solution.py
+++ b/solution.py
@@ -11,6 +11,7 @@
 PLANES = 4
 CHUNKS = 4
 TILE = 256
+SPAN = 5
 
 
 def gated(gate, up):
@@ -125,27 +126,19 @@
             own(r, h).wait()
         forward(z, True, r)
 
-    def product(s, first, count, j):
-        lhs = x[order[s], pl.ds(first, count), :]
-        cut = pl.ds(pl.multiple_of(j * TILE, TILE), TILE)
-        gate = jnp.dot(lhs, bg[s % 2, :, cut], preferred_element_type=jnp.float32)
-        up = jnp.dot(lhs, bu[s % 2, :, cut], preferred_element_type=jnp.float32)
-        return gate, up
-
-    def accumulate(s, first, count):
+    def accumulate(s, first, count, span):
         here = pl.ds(first, count)
-
-        def body(j, carry):
-            gate, up = product(s, first, count, j)
+        for j in span:
+            lhs = x[order[s], here, :]
+            cut = pl.ds(j * TILE, TILE)
+            gate = jnp.dot(lhs, bg[s % 2, :, cut], preferred_element_type=jnp.float32)
+            up = jnp.dot(lhs, bu[s % 2, :, cut], preferred_element_type=jnp.float32)
             if s:
                 acc[j, here, :TILE] += gate
                 acc[j, here, TILE:] += up
             else:
                 acc[j, here, :TILE] = gate
                 acc[j, here, TILE:] = up
-            return carry
-
-        lax.fori_loop(0, tiles, body, 0)
 
     def exchange(r, j):
         return pltpu.make_async_remote_copy(
@@ -187,7 +180,7 @@
             def block(k, carry, s=s):
                 for i in range(group):
                     chunk(k * group + i, 0, s)
-                accumulate(s, pl.multiple_of(k * group * size, size), group * size)
+                accumulate(s, pl.multiple_of(k * group * size, size), group * size, range(tiles))
                 return carry
 
             lax.fori_loop(0, CHUNKS // group, block, 0)
@@ -197,13 +190,14 @@
         else:
             def last(r, carry, s=s):
                 chunk(r, 0, s)
-                accumulate(s, pl.multiple_of(r * size, size), size)
-
                 def push(j, carry):
                     exchange(r, j).start()
                     return carry
 
-                lax.fori_loop(0, tiles, push, 0)
+                for lo in range(0, tiles, SPAN):
+                    hi = min(lo + SPAN, tiles)
+                    accumulate(s, pl.multiple_of(r * size, size), size, range(lo, hi))
+                    lax.fori_loop(lo, hi, push, 0)
 
                 @pl.when(r > 0)
                 def _():

time: 80.2 us -> 66.5 us (0.83)
  Pallas kernels: 77.3 us -> 63.6 us
    pallas_call x1, Pallas kernels: 77.3 us -> 63.6 us  [fused(): pl.pallas_call(kernel, out_shape=jax.ShapeDtypeStruct((rows // 2, hidden)...]
where the time goes in v2:
time: 66.5 us; the launch traced here: 66.3 us
  Pallas kernels  63.6 us (96%)
  local copies, waits for them, and re-layouts  2.75 us (4%)
    pallas_call x1, Pallas kernels, fused(): pl.pallas_call(kernel, out_shape=jax.ShapeDtypeStruct((rows // 2, hidden)...  63.6 us
    unnamed x1, local copies, waits for them, and re-layouts  2.75 us

profile of v2, /device:TPU:1, one launch (start us, length us, event | category | flops | bytes accessed | tf_op | source)
XLA Modules:
  0.0 66.3 jit_solution(3472252019412548821)
XLA Ops:
  0.0 63.6 %shard_map.37 = bf16[256,3328]{1,0:T(8,128)(2,1)} custom-call(bf16[512,512]{1,0:T(8,128)(2,1)} %bitcast.1, bf16[4096,3328]{1,0:T(8,128)(2,1)} %wg.1, bf16[4096,3328]{1,0:T(8,128)(2,1)} %wu.1), custom_call_target="tpu_custom_call" | custom-call | flops 27917287424 | bytes 54525952 | tf_op jit(solution)/shard_map/pallas_call | solution.py:231
  63.6 2.7 %copy.5 = bf16[256,3328]{1,0:T(8,128)(2,1)} copy(bf16[256,3328]{1,0:T(8,128)(2,1)} %shard_map.37) | data formatting | bytes 3407872

commit v3 on v2

--- a/solution.py
+++ b/solution.py
@@ -163,7 +163,7 @@
         lax.fori_loop(0, tiles, body, 0)
         write(r).start()
 
-    group = 2
+    group = 1
     for s in range(PLANES):
         for copy in weights(s):
             copy.wait()

time: 66.5 us -> 65.1 us (0.979)
  Pallas kernels: 63.6 us -> 62.2 us
    pallas_call x1, Pallas kernels: 63.6 us -> 62.2 us  [fused(): pl.pallas_call(kernel, out_shape=jax.ShapeDtypeStruct((rows // 2, hidden)...]
where the time goes in v3:
time: 65.1 us; the launch traced here: 64.9 us
  Pallas kernels  62.2 us (96%)
  local copies, waits for them, and re-layouts  2.75 us (4%)
    pallas_call x1, Pallas kernels, fused(): pl.pallas_call(kernel, out_shape=jax.ShapeDtypeStruct((rows // 2, hidden)...  62.2 us
    unnamed x1, local copies, waits for them, and re-layouts  2.75 us

profile of v3, /device:TPU:1, one launch (start us, length us, event | category | flops | bytes accessed | tf_op | source)
XLA Modules:
  0.0 64.9 jit_solution(1305630932528152298)
XLA Ops:
  0.0 62.2 %shard_map.37 = bf16[256,3328]{1,0:T(8,128)(2,1)} custom-call(bf16[512,512]{1,0:T(8,128)(2,1)} %bitcast.1, bf16[4096,3328]{1,0:T(8,128)(2,1)} %wg.1, bf16[4096,3328]{1,0:T(8,128)(2,1)} %wu.1), custom_call_target="tpu_custom_call" | custom-call | flops 27917287424 | bytes 54525952 | tf_op jit(solution)/shard_map/pallas_call | solution.py:231
  62.2 2.7 %copy.5 = bf16[256,3328]{1,0:T(8,128)(2,1)} copy(bf16[256,3328]{1,0:T(8,128)(2,1)} %shard_map.37) | data formatting | bytes 3407872
